TPU v7x, 32 devices: a whole 2x2x4 slice. The times are simulated.
32 devices in a mesh: section: 2 (over x), dp: 16 (over z, y, core).
Axes of the slice: x: 2, y: 2, z: 4, core: 2. Of those that a mesh axis runs over, the one named last changes fastest.
Arguments:
- tokens: bfloat16 [32768, 768], P('dp'), may hold values from -6 to 6
- cotangent: bfloat16 [32768, 768], P('dp'), may hold values from -6 to 6
- segment_ids: int32 [64, 512], P('dp'), may hold values from 0 to 7, never falling along the last dimension, each value on 1 to 128 neighbouring positions
- feature_ids: int32 [64, 512], P('dp'), may hold values from 0 to 127, never falling along the last dimension, each value on 1 to 8 neighbouring positions
- w_qkv: bfloat16 [2, 768, 2304], P('section'), may hold values from -0.21875 to 0.21875
- w_out: bfloat16 [2, 768, 768], P('section'), may hold values from -0.875 to 0.875
- gain_attn: float32 [2, 768], P('section'), may hold values from 0.5 to 1.5
- shift_attn: float32 [2, 768], P('section'), may hold values from -3 to 3
- w_up: bfloat16 [2, 768, 3072], P('section'), may hold values from -0.21875 to 0.21875
- bias_up: float32 [2, 3072], P('section'), may hold values from -3 to 3
- w_down: bfloat16 [2, 3072, 768], P('section'), may hold values from -0.109375 to 0.109375
- bias_down: float32 [2, 768], P('section'), may hold values from -3 to 3
- gain_ffn: float32 [2, 768], P('section'), may hold values from 0.5 to 1.5
- shift_ffn: float32 [2, 768], P('section'), may hold values from -3 to 3
Outputs:
- activations: bfloat16 [2, 32768, 768], P('section', 'dp')
- input_grads: bfloat16 [2, 32768, 768], P('section', 'dp')
- grad_w_qkv: float32 [2, 768, 2304], P('section', 'dp')
- grad_w_out: float32 [2, 768, 768], P('section', 'dp')
- grad_gain_attn: float32 [2, 768], P('section', 'dp')
- grad_shift_attn: float32 [2, 768], P('section', 'dp')
- grad_w_up: float32 [2, 768, 3072], P('section', 'dp')
- grad_bias_up: float32 [2, 3072], P('section', 'dp')
- grad_w_down: float32 [2, 3072, 768], P('section', 'dp')
- grad_bias_down: float32 [2, 768], P('section', 'dp')
- grad_gain_ffn: float32 [2, 768], P('section', 'dp')
- grad_shift_ffn: float32 [2, 768], P('section', 'dp')
All inputs are finite; a program needn't handle non-finite values.
Results may differ from a plain program's by a relative error of at most 0.02.
Values may be sent and summed in bfloat16 or wider, within the bound.
A program may use at most 512 MiB of HBM per device.

v0:
```python
import jax
import jax.numpy as jnp
from jax import lax
from jax.sharding import PartitionSpec as P

HEAD_DIM = 64
MICRO = 4


norm_eps = 1e-05
head_scale = 0.125
masked_score = -1e30


def from_behind(value, axis, steps):
    count = lax.axis_size(axis)
    first, last = (max(0, -steps), min(count, count - steps))
    return lax.ppermute(value, axis, [(source, source + steps) for source in range(first, last)])


def norm_forward(values, gain_row, shift_row):
    centre = values - jnp.mean(values, axis=-1, keepdims=True)
    inverse = lax.rsqrt(jnp.mean(centre * centre, axis=-1, keepdims=True) + norm_eps)
    normed = centre * inverse
    return (normed * gain_row + shift_row, normed, inverse)


def norm_backward(grad_rows, normed, inverse, gain_row):
    scaled = grad_rows * gain_row
    inner_term = (
        scaled
        - jnp.mean(scaled, axis=-1, keepdims=True)
        - normed * jnp.mean(scaled * normed, axis=-1, keepdims=True)
    )
    return (inverse * inner_term, jnp.sum(grad_rows * normed, axis=0), jnp.sum(grad_rows, axis=0))


def weight_product(left_side, right_side):
    return lax.dot_general(
        left_side, right_side, (((0,), (0,)), ((), ())), preferred_element_type=jnp.float32
    )


def transpose_product(left_side, right_side):
    return lax.dot_general(
        left_side, right_side, (((1,), (1,)), ((), ())), preferred_element_type=jnp.float32
    )


def score_block(queries, key_heads, segments, groups):
    same_seg = segments[:, :, None] == segments[:, None, :]
    same_group = groups[:, :, None] == groups[:, None, :]
    allowed = (same_seg & same_group)[:, None, :, :]
    raw_scores = (
        jnp.einsum("bqhe,bkhe->bhqk", queries, key_heads, preferred_element_type=jnp.float32)
        * head_scale
    )
    return jnp.where(allowed, raw_scores, masked_score)


def split_heads(qkv_rows, seq_count, seq_len):
    head_count = qkv_rows.shape[1] // (3 * HEAD_DIM)
    head_parts = qkv_rows.reshape(seq_count, seq_len, 3, head_count, HEAD_DIM)
    return (head_parts[:, :, 0], head_parts[:, :, 1], head_parts[:, :, 2])


def layer_forward(inputs, segments, groups, weights):
    w_qkv, w_out, gain_attn, shift_attn, w_up, bias_up, w_down, bias_down, gain_ffn, shift_ffn = (
        weights
    )
    seq_count, seq_len = segments.shape
    model_width = inputs.shape[1]
    qkv_rows = jnp.dot(inputs, w_qkv, preferred_element_type=jnp.float32).astype(jnp.bfloat16)
    queries, key_heads, value_heads = split_heads(qkv_rows, seq_count, seq_len)
    scores = score_block(queries, key_heads, segments, groups)
    row_top = jnp.max(scores, axis=-1, keepdims=True)
    exponent = jnp.exp(scores - row_top)
    row_total = jnp.sum(exponent, axis=-1, keepdims=True)
    prob_low = (exponent / row_total).astype(jnp.bfloat16)
    log_total = row_top + jnp.log(row_total)
    context = jnp.einsum(
        "bhqk,bkhe->bqhe", prob_low, value_heads, preferred_element_type=jnp.float32
    )
    context = context.astype(jnp.bfloat16).reshape(-1, model_width)
    attn_sum = inputs.astype(jnp.float32) + jnp.dot(
        context, w_out, preferred_element_type=jnp.float32
    )
    normed_attn, normed_one, inverse_one = norm_forward(attn_sum, gain_attn, shift_attn)
    normed_low = normed_attn.astype(jnp.bfloat16)
    pre_act = jnp.dot(normed_low, w_up, preferred_element_type=jnp.float32) + bias_up
    activated = jax.nn.gelu(pre_act).astype(jnp.bfloat16)
    ffn_sum = (
        normed_attn + jnp.dot(activated, w_down, preferred_element_type=jnp.float32) + bias_down
    )
    output, normed_two, inverse_two = norm_forward(ffn_sum, gain_ffn, shift_ffn)
    kept_state = (
        inputs,
        qkv_rows,
        log_total,
        context,
        normed_one,
        inverse_one,
        normed_low,
        pre_act,
        activated,
        normed_two,
        inverse_two,
    )
    return (output.astype(jnp.bfloat16), kept_state)


def layer_backward(grad_out, kept_state, segments, groups, weights):
    w_qkv, w_out, gain_attn, shift_attn, w_up, bias_up, w_down, bias_down, gain_ffn, shift_ffn = (
        weights
    )
    (
        inputs,
        qkv_rows,
        log_total,
        context,
        normed_one,
        inverse_one,
        normed_low,
        pre_act,
        activated,
        normed_two,
        inverse_two,
    ) = kept_state
    seq_count, seq_len = segments.shape
    model_width = inputs.shape[1]
    d_ffn, grad_gain_ffn, grad_shift_ffn = norm_backward(
        grad_out.astype(jnp.float32), normed_two, inverse_two, gain_ffn
    )
    down_in = d_ffn.astype(jnp.bfloat16)
    grad_bias_down = jnp.sum(down_in.astype(jnp.float32), axis=0)
    d_activated = transpose_product(down_in, w_down)
    unused_value, gelu_back = jax.vjp(jax.nn.gelu, pre_act)
    up_in = gelu_back(d_activated)[0].astype(jnp.bfloat16)
    grad_bias_up = jnp.sum(up_in.astype(jnp.float32), axis=0)
    d_normed = d_ffn + transpose_product(up_in, w_up)
    d_attn, grad_gain_attn, grad_shift_attn = norm_backward(
        d_normed, normed_one, inverse_one, gain_attn
    )
    out_in = d_attn.astype(jnp.bfloat16)
    head_count = model_width // HEAD_DIM
    d_context = (
        transpose_product(out_in, w_out)
        .astype(jnp.bfloat16)
        .reshape(seq_count, seq_len, head_count, HEAD_DIM)
    )
    queries, key_heads, value_heads = split_heads(qkv_rows, seq_count, seq_len)
    scores = score_block(queries, key_heads, segments, groups)
    prob_full = jnp.exp(scores - log_total)
    prob_low = prob_full.astype(jnp.bfloat16)
    d_values = jnp.einsum(
        "bhqk,bqhe->bkhe", prob_low, d_context, preferred_element_type=jnp.float32
    ).astype(jnp.bfloat16)
    d_prob = jnp.einsum(
        "bqhe,bkhe->bhqk", d_context, value_heads, preferred_element_type=jnp.float32
    )
    d_score = (prob_full * (d_prob - jnp.sum(d_prob * prob_full, axis=-1, keepdims=True))).astype(
        jnp.bfloat16
    )
    d_queries = (
        jnp.einsum("bhqk,bkhe->bqhe", d_score, key_heads, preferred_element_type=jnp.float32)
        * head_scale
    ).astype(jnp.bfloat16)
    d_keys = (
        jnp.einsum("bhqk,bqhe->bkhe", d_score, queries, preferred_element_type=jnp.float32)
        * head_scale
    ).astype(jnp.bfloat16)
    d_qkv = jnp.stack([d_queries, d_keys, d_values], axis=2).reshape(-1, 3 * model_width)
    d_inputs = (d_attn + transpose_product(d_qkv, w_qkv)).astype(jnp.bfloat16)
    small_grads = (
        grad_gain_attn,
        grad_shift_attn,
        grad_bias_up,
        grad_bias_down,
        grad_gain_ffn,
        grad_shift_ffn,
    )
    grad_rows = (down_in, up_in, out_in, d_qkv)
    return (d_inputs, small_grads, grad_rows)


def body(
    tokens,
    cotangent,
    segment_ids,
    feature_ids,
    w_qkv,
    w_out,
    gain_attn,
    shift_attn,
    w_up,
    bias_up,
    w_down,
    bias_down,
    gain_ffn,
    shift_ffn,
):
    section_index = lax.axis_index("section")
    weights = (
        w_qkv[0],
        w_out[0],
        gain_attn[0],
        shift_attn[0],
        w_up[0],
        bias_up[0],
        w_down[0],
        bias_down[0],
        gain_ffn[0],
        shift_ffn[0],
    )
    model_width = tokens.shape[1]
    micro_rows = tokens.shape[0] // MICRO
    seq_len = segment_ids.shape[1]
    per_micro = segment_ids.shape[0] // MICRO
    inputs_all = tokens.reshape(MICRO, micro_rows, model_width)
    cotangent_all = cotangent.reshape(MICRO, micro_rows, model_width)
    segs_all = segment_ids.reshape(MICRO, per_micro, seq_len)
    groups_all = (feature_ids * (1 - section_index)).reshape(MICRO, per_micro, seq_len)
    kept_store = None
    output_store = jnp.zeros((MICRO, micro_rows, model_width), jnp.bfloat16)
    incoming = jnp.zeros((micro_rows, model_width), jnp.bfloat16)
    for tick_number in range(MICRO + 1):
        slot_index = jnp.clip(tick_number - section_index, 0, MICRO - 1)
        own_rows = inputs_all[min(tick_number, MICRO - 1)]
        layer_in = jnp.where(section_index == 0, own_rows, incoming)
        segments = lax.dynamic_index_in_dim(segs_all, slot_index, 0, keepdims=False)
        groups = lax.dynamic_index_in_dim(groups_all, slot_index, 0, keepdims=False)
        layer_out, kept_state = layer_forward(layer_in, segments, groups, weights)
        if kept_store is None:
            kept_store = jax.tree.map(
                lambda leaf_array: jnp.zeros((MICRO,) + leaf_array.shape, leaf_array.dtype),
                kept_state,
            )
        kept_store = jax.tree.map(
            lambda store_array, leaf_array: lax.dynamic_update_index_in_dim(
                store_array, leaf_array, slot_index, 0
            ),
            kept_store,
            kept_state,
        )
        output_store = lax.dynamic_update_index_in_dim(output_store, layer_out, slot_index, 0)
        if tick_number < MICRO:
            incoming = from_behind(layer_out, "section", 1)
    small_totals = None
    big_totals = None
    input_store = jnp.zeros((MICRO, micro_rows, model_width), jnp.bfloat16)
    incoming = jnp.zeros((micro_rows, model_width), jnp.bfloat16)
    for tick_number in range(MICRO + 1):
        raw_index = tick_number - 1 + section_index
        slot_index = jnp.clip(raw_index, 0, MICRO - 1)
        valid_flag = ((raw_index >= 0) & (raw_index < MICRO)).astype(jnp.float32)
        own_rows = cotangent_all[min(tick_number, MICRO - 1)]
        grad_in = jnp.where(section_index == 1, own_rows, incoming)
        kept_state = jax.tree.map(
            lambda store_array: lax.dynamic_index_in_dim(
                store_array, slot_index, 0, keepdims=False
            ),
            kept_store,
        )
        segments = lax.dynamic_index_in_dim(segs_all, slot_index, 0, keepdims=False)
        groups = lax.dynamic_index_in_dim(groups_all, slot_index, 0, keepdims=False)
        d_inputs, small_grads, grad_rows = layer_backward(
            grad_in, kept_state, segments, groups, weights
        )
        input_store = lax.dynamic_update_index_in_dim(input_store, d_inputs, slot_index, 0)
        if tick_number < MICRO:
            incoming = from_behind(d_inputs, "section", -1)
        small_grads = tuple((entry * valid_flag for entry in small_grads))
        if small_totals is None:
            small_totals = small_grads
        else:
            small_totals = tuple(
                (running + entry for running, entry in zip(small_totals, small_grads))
            )
        down_in, up_in, out_in, d_qkv = grad_rows
        big_grads = (
            weight_product(kept_state[0], d_qkv),
            weight_product(kept_state[3], out_in),
            weight_product(kept_state[6], up_in),
            weight_product(kept_state[8], down_in),
        )
        big_grads = tuple((entry * valid_flag for entry in big_grads))
        if big_totals is None:
            big_totals = big_grads
        else:
            big_totals = tuple((running + entry for running, entry in zip(big_totals, big_grads)))
    grad_gain_attn, grad_shift_attn, grad_bias_up, grad_bias_down, grad_gain_ffn, grad_shift_ffn = (
        small_totals
    )
    grad_w_qkv, grad_w_out, grad_w_up, grad_w_down = big_totals
    summed = (
        lax.psum_scatter(grad_w_qkv, "dp", scatter_dimension=0, tiled=True),
        lax.psum_scatter(grad_w_out, "dp", scatter_dimension=0, tiled=True),
        lax.psum_scatter(grad_gain_attn, "dp", scatter_dimension=0, tiled=True),
        lax.psum_scatter(grad_shift_attn, "dp", scatter_dimension=0, tiled=True),
        lax.psum_scatter(grad_w_up, "dp", scatter_dimension=0, tiled=True),
        lax.psum_scatter(grad_bias_up, "dp", scatter_dimension=0, tiled=True),
        lax.psum_scatter(grad_w_down, "dp", scatter_dimension=0, tiled=True),
        lax.psum_scatter(grad_bias_down, "dp", scatter_dimension=0, tiled=True),
        lax.psum_scatter(grad_gain_ffn, "dp", scatter_dimension=0, tiled=True),
        lax.psum_scatter(grad_shift_ffn, "dp", scatter_dimension=0, tiled=True),
    )
    activations = output_store.reshape(1, MICRO * micro_rows, model_width)
    input_grads = input_store.reshape(1, MICRO * micro_rows, model_width)
    shards = tuple((entry[None] for entry in summed))
    return (activations, input_grads) + shards


def solution(mesh):
    in_specs = (
        P("dp", None),
        P("dp", None),
        P("dp", None),
        P("dp", None),
        P("section", None, None),
        P("section", None, None),
        P("section", None),
        P("section", None),
        P("section", None, None),
        P("section", None),
        P("section", None, None),
        P("section", None),
        P("section", None),
        P("section", None),
    )
    out_specs = (
        P("section", "dp", None),
        P("section", "dp", None),
        P("section", "dp", None),
        P("section", "dp", None),
        P("section", "dp"),
        P("section", "dp"),
        P("section", "dp", None),
        P("section", "dp"),
        P("section", "dp", None),
        P("section", "dp"),
        P("section", "dp"),
        P("section", "dp"),
    )
    return jax.shard_map(body, mesh=mesh, in_specs=in_specs, out_specs=out_specs, check_vma=False)
```

profile of v0, /device:TPU:0, one launch (start us, length us, event | category | flops | bytes accessed | tf_op | source)
XLA Modules:
  0.0 1123.2 jit_solution(3508417932941078973)
XLA Ops:
  44.5 11.5 %broadcast_in_dim.399 = f32[4,512,3072]{2,1,0:T(8,128)} broadcast(f32[]{:T(128)} %constant.404.clone.1), dimensions={} | broadcast | bytes 25165828 | tf_op jit(solution)/shard_map/broadcast_in_dim | solution.py:235
  63.3 8.8 fusion.509
  135.8 8.2 bitcast_dynamic-update-slice_fusion.3
  193.6 8.2 bitcast_dynamic-update-slice_fusion.2
  254.0 8.1 bitcast_dynamic-update-slice_fusion.1
  313.5 8.4 bitcast_dynamic-update-slice_fusion
  337.8 9.4 convert_reduce_fusion.4
  358.2 9.0 constant_dynamic-slice_fusion.3
  474.5 9.4 convert_reduce_fusion.3
  501.1 9.7 multiply_reduce_fusion.3
  536.6 8.4 collective-permute-done.5
  550.7 9.8 convert_reduce_fusion.2
  577.7 9.8 multiply_reduce_fusion.2
  625.7 9.5 convert_reduce_fusion.1
  652.4 9.7 multiply_reduce_fusion.1
  699.7 9.4 convert_reduce_fusion
  725.5 13.7 %multiply_reduce_fusion = (f32[12,512]{1,0:T(8,128)S(1)}, f32[12,512,512]{1,2,0:T(8,128)}) fusion(f32[12,512,512]{1,2,0:T(8,128)} %fusion.425, f32[12,512]{1,0:T(8,128)} %get-tuple-element.93, pred[512,512]{0,1:T(8,128)(4,1)} %compare_and_fusion, bf16[512,12,64]{0,2,1:T(8,128)(2,1)} %bitcast.980, bf16[1,512,3,12,64]{1,4,3,2,0:T(8,128)(2,1)} %bitcast.934), kind=kOutput, calls=%fused_computation.1 | convolution fusion | flops 418375680 | bytes 27058176 | tf_op jit(solution)/shard_map/bqhe,bkhe->bhqk/dot_general | solution.py:158
  754.9 14.2 %multiply_add_fusion.2 = f32[768,2304]{1,0:T(8,128)} fusion(f32[768,2304]{1,0:T(8,128)} %fusion.398, f32[768,2304]{1,0:T(8,128)} %fusion.400, f32[768,2304]{1,0:T(8,128)} %fusion.402, f32[768,2304]{1,0:T(8,128)} %fusion.404, bf16[512,2304]{0,1:T(8,128)(2,1)S(1)} %bitcast.954, f32[]{:T(128)S(6)} %convert_element_type.588, f32[]{:T(128)S(6)} %convert_element_type.587, ...), kind=kOutput, calls=%fused_computation.57 | convolution fusion | flops 1827864576 | bytes 38535192 | tf_op jit(solution)/shard_map/dot_general | solution.py:39
  795.3 23.9 %multiply_add_fusion.1 = f32[768,3072]{1,0:T(8,128)} fusion(f32[768,3072]{1,0:T(8,128)} %fusion.380, f32[768,3072]{1,0:T(8,128)} %fusion.382, f32[768,3072]{1,0:T(8,128)} %fusion.384, f32[768,3072]{1,0:T(8,128)} %fusion.386, bf16[512,3072]{1,0:T(8,128)(2,1)} %copy-done.62, f32[]{:T(128)S(6)} %convert_element_type.588, f32[]{:T(128)S(6)} %convert_element_type.587, ...), kind=kOutput, calls=%fused_computation.46 | convolution fusion | flops 2437152768 | bytes 51118104 | tf_op jit(solution)/shard_map/dot_general | solution.py:39
  847.4 8.3 fusion.182
  871.3 21.3 %multiply_add_fusion = f32[3072,768]{1,0:T(8,128)} fusion(f32[3072,768]{1,0:T(8,128)} %fusion.176, f32[3072,768]{1,0:T(8,128)} %fusion.178, f32[3072,768]{1,0:T(8,128)} %fusion.180, f32[3072,768]{1,0:T(8,128)} %fusion.182, f32[]{:T(128)S(6)} %convert_element_type.588, f32[]{:T(128)S(6)} %convert_element_type.587, f32[]{:T(128)S(6)} %convert_element_type.586, ...), kind=kOutput, calls=%fused_computation.45 | convolution fusion | flops 2437545984 | bytes 51904536 | tf_op jit(solution)/shard_map/dot_general | solution.py:39
  904.7 62.0 %all-reduce.6 = (f32[768]{0:T(1024)}, f32[768]{0:T(1024)}, f32[3072]{0:T(1024)}, f32[768]{0:T(1024)}, f32[768]{0:T(1024)}, /*index=5*/f32[768]{0:T(1024)}) all-reduce(f32[768]{0:T(1024)S(1)} %multiply_add_fusion.14, f32[768]{0:T(1024)} %multiply_add_fusion.13, ...), channel_id=4, replica_groups=mesh['section'=2,'dp'=16] {'dp'}, use_global_device_ids=true, to_apply=%region_62.63.clone | all-reduce | flops 6912 | bytes 55296
  979.4 20.8 %reduce-scatter.9.cloned.1.call-done = f32[48,3072]{1,0:T(8,128)} async-done(((f32[768,3072]{1,0:T(8,128)}), f32[48,3072]{1,0:T(8,128)}) %reduce-scatter.9.cloned.1.call-update) | async-done | bytes 589840 | tf_op jit(solution)/shard_map/reduce_scatter | solution.py:300
  1000.2 116.2 %reduce-scatter.11.cloned.1.call-done = f32[192,768]{1,0:T(8,128)} async-done(((f32[3072,768]{1,0:T(8,128)}), f32[192,768]{1,0:T(8,128)}) %reduce-scatter.11.cloned.1.call-update) | async-done | bytes 589840 | tf_op jit(solution)/shard_map/reduce_scatter | solution.py:302
  (824 shorter events, 677.3 us)
Async XLA Ops:
  7.2 972.2 %reduce-scatter.7.cloned.1.call-start = ((), (), s32[]{:S(2)}) async-start(), calls=%async_computation.5 | async-start | bytes 2506752 | tf_op jit(solution)/shard_map/reduce_scatter | solution.py:297
  8.1 258.7 %copy-start.108 = (f32[768]{0:T(1024)}, f32[768]{0:T(1024)S(1)}, u32[]{:S(2)}) copy-start(f32[768]{0:T(1024)S(1)} %reduce.34) | copy-start | bytes 9220
  9.0 688.2 %copy-start.80 = (f32[768]{0:T(1024)}, f32[768]{0:T(1024)S(1)}, u32[]{:S(2)}) copy-start(f32[768]{0:T(1024)S(1)} %reduce.33) | copy-start | bytes 9220
  40.7 281.1 %copy-start.110 = (f32[768]{0:T(1024)}, f32[768]{0:T(1024)S(1)}, u32[]{:S(2)}) copy-start(f32[768]{0:T(1024)S(1)} %reduce.31) | copy-start | bytes 9220
  44.5 53.5 %copy-start.138 = (f32[512]{0:T(512)}, f32[512]{0:T(512)S(1)}, u32[]{:S(2)}) copy-start(f32[512]{0:T(512)S(1)} %add_rsqrt_fusion.9) | copy-start | bytes 6148
  76.1 20.3 %copy-start.158 = (s32[1,512]{1,0:T(1,128)S(1)}, s32[1,512]{1,0:T(1,128)}, u32[]{:S(2)}) copy-start(s32[1,512]{1,0:T(1,128)} %get-tuple-element.108) | copy-start | bytes 6148
  76.1 35.3 %collective-permute-start = (bf16[512,768]{1,0:T(8,128)(2,1)}, bf16[512,768]{1,0:T(8,128)(2,1)}, u32[]{:S(2)}, u32[]{:S(2)}) collective-permute-start(bf16[512,768]{1,0:T(8,128)(2,1)} %get-tuple-element.87), channel_id=1, source_target_pairs={{0,16},{1,17},{2,18},{3,19},{4,20},{5,21},{6,22},{7,23},{8,24},{9,... | collective-permute-start | bytes 2359304 | tf_op jit(solution)/shard_map/ppermute | solution.py:18
  150.9 18.4 %collective-permute-start.1 = (bf16[512,768]{1,0:T(8,128)(2,1)}, bf16[512,768]{1,0:T(8,128)(2,1)}, u32[]{:S(2)}, u32[]{:S(2)}) collective-permute-start(bf16[512,768]{1,0:T(8,128)(2,1)} %get-tuple-element.85), channel_id=1, source_target_pairs={{0,16},{1,17},{2,18},{3,19},{4,20},{5,21},{6,22},{7,23},{8,24},{9,... | collective-permute-start | bytes 2359304 | tf_op jit(solution)/shard_map/ppermute | solution.py:18
  193.5 21.9 %copy-start.142 = (f32[512]{0:T(512)}, f32[512]{0:T(512)S(1)}, u32[]{:S(2)}) copy-start(f32[512]{0:T(512)S(1)} %add_rsqrt_fusion.5) | copy-start | bytes 6148
  208.6 20.9 %collective-permute-start.2 = (bf16[512,768]{1,0:T(8,128)(2,1)}, bf16[512,768]{1,0:T(8,128)(2,1)}, u32[]{:S(2)}, u32[]{:S(2)}) collective-permute-start(bf16[512,768]{1,0:T(8,128)(2,1)} %get-tuple-element.83), channel_id=1, source_target_pairs={{0,16},{1,17},{2,18},{3,19},{4,20},{5,21},{6,22},{7,23},{8,24},{9,... | collective-permute-start | bytes 2359304 | tf_op jit(solution)/shard_map/ppermute | solution.py:18
  254.0 21.9 %copy-start.146 = (f32[512]{0:T(512)}, f32[512]{0:T(512)S(1)}, u32[]{:S(2)}) copy-start(f32[512]{0:T(512)S(1)} %add_rsqrt_fusion.3) | copy-start | bytes 6148
  269.1 20.0 %collective-permute-start.3 = (bf16[512,768]{1,0:T(8,128)(2,1)}, bf16[512,768]{1,0:T(8,128)(2,1)}, u32[]{:S(2)}, u32[]{:S(2)}) collective-permute-start(bf16[512,768]{1,0:T(8,128)(2,1)} %get-tuple-element.81), channel_id=1, source_target_pairs={{0,16},{1,17},{2,18},{3,19},{4,20},{5,21},{6,22},{7,23},{8,24},{9,... | collective-permute-start | bytes 2359304 | tf_op jit(solution)/shard_map/ppermute | solution.py:18
  313.4 37.4 %copy-start.148 = (f32[512]{0:T(512)}, f32[512]{0:T(512)S(1)}, u32[]{:S(2)}) copy-start(f32[512]{0:T(512)S(1)} %add_rsqrt_fusion.1) | copy-start | bytes 6148
  326.7 26.0 %copy-start.3 = (f32[4,512,768]{2,1,0:T(8,128)}, f32[4,512,768]{2,1,0:T(8,128)S(1)}, u32[]{:S(2)}) copy-start(f32[4,512,768]{2,1,0:T(8,128)S(1)} %bitcast_dynamic-update-slice_fusion.15) | copy-start | bytes 18874372
  404.8 63.8 %collective-permute-start.4 = (bf16[512,768]{1,0:T(8,128)(2,1)}, bf16[512,768]{1,0:T(8,128)(2,1)}, u32[]{:S(2)}, u32[]{:S(2)}) collective-permute-start(bf16[512,768]{1,0:T(8,128)(2,1)} %get-tuple-element.182), channel_id=1, source_target_pairs={{16,0},{17,1},{18,2},{19,3},{20,4},{21,5},{22,6},{23,7},{24,8},{25... | collective-permute-start | bytes 2359304 | tf_op jit(solution)/shard_map/ppermute | solution.py:18
  525.6 19.4 %collective-permute-start.5 = (bf16[512,768]{1,0:T(8,128)(2,1)S(1)}, bf16[512,768]{1,0:T(8,128)(2,1)S(1)}, u32[]{:S(2)}, u32[]{:S(2)}) collective-permute-start(bf16[512,768]{1,0:T(8,128)(2,1)S(1)} %get-tuple-element.187), channel_id=1, source_target_pairs={{16,0},{17,1},{18,2},{19,3},{20,4},{21,5},{22,6},{23,7},{24,8},{25... | collective-permute-start | bytes 2359304 | tf_op jit(solution)/shard_map/ppermute | solution.py:18
  526.9 23.7 %slice-start.38 = ((s8[4718592]{0:T(1024)(128)(4,1)}), s8[4194304]{0:T(1024)(128)(4,1)S(1)}, s32[]{:S(2)}) async-start(s8[4718592]{0:T(1024)(128)(4,1)} %bitcast.1068), calls=%async_computation.46 | async-start | bytes 8388608
  602.3 17.8 %collective-permute-start.6 = (bf16[512,768]{1,0:T(8,128)(2,1)S(1)}, bf16[512,768]{1,0:T(8,128)(2,1)S(1)}, u32[]{:S(2)}, u32[]{:S(2)}) collective-permute-start(bf16[512,768]{1,0:T(8,128)(2,1)S(1)} %get-tuple-element.192), channel_id=1, source_target_pairs={{16,0},{17,1},{18,2},{19,3},{20,4},{21,5},{22,6},{23,7},{24,8},{25... | collective-permute-start | bytes 2359304 | tf_op jit(solution)/shard_map/ppermute | solution.py:18
  603.6 22.1 %slice-start.40 = ((s8[4718592]{0:T(1024)(128)(4,1)}), s8[4194304]{0:T(1024)(128)(4,1)S(1)}, s32[]{:S(2)}) async-start(s8[4718592]{0:T(1024)(128)(4,1)} %bitcast.1070), calls=%async_computation.48 | async-start | bytes 8388608
  677.2 16.9 %collective-permute-start.7 = (bf16[512,768]{1,0:T(8,128)(2,1)S(1)}, bf16[512,768]{1,0:T(8,128)(2,1)S(1)}, u32[]{:S(2)}, u32[]{:S(2)}) collective-permute-start(bf16[512,768]{1,0:T(8,128)(2,1)S(1)} %get-tuple-element.197), channel_id=1, source_target_pairs={{16,0},{17,1},{18,2},{19,3},{20,4},{21,5},{22,6},{23,7},{24,8},{25... | collective-permute-start | bytes 2359304 | tf_op jit(solution)/shard_map/ppermute | solution.py:18
  678.5 21.2 %slice-start.42 = ((s8[4718592]{0:T(1024)(128)(4,1)}), s8[4194304]{0:T(1024)(128)(4,1)S(1)}, s32[]{:S(2)}) async-start(s8[4718592]{0:T(1024)(128)(4,1)} %bitcast.1072), calls=%async_computation.50 | async-start | bytes 8388608
  725.4 254.0 %reduce-scatter.5.cloned.1.call-start = ((), (), s32[]{:S(2)}) async-start(), calls=%async_computation.4 | async-start | bytes 7520256 | tf_op jit(solution)/shard_map/reduce_scatter | solution.py:296
  769.2 231.1 %reduce-scatter.9.cloned.1.call-start = ((), (), s32[]{:S(2)}) async-start(), calls=%async_computation.6 | async-start | bytes 10027008 | tf_op jit(solution)/shard_map/reduce_scatter | solution.py:300
  819.3 297.1 %reduce-scatter.11.cloned.1.call-start = ((), (), s32[]{:S(2)}) async-start(), calls=%async_computation.7 | async-start | bytes 10027008 | tf_op jit(solution)/shard_map/reduce_scatter | solution.py:302
  (239 other events, 1825.2 us)
Sparse Core Ops, SparseCore 0:
  725.5 63.2 reduce-scatter.6
  794.0 89.0 reduce-scatter.4
  887.7 112.4 reduce-scatter.8
  1005.3 111.1 reduce-scatter.10
where the time goes:
time: 1130 us; the launch traced here: 1120 us
  matrix products  508 us (45%)
  waiting for transfers between devices  173 us (15%)
  other arithmetic  172 us (15%)
  local copies, waits for them, and re-layouts  166 us (15%)
  blocking collectives  62 us (5%)
  starting transfers between devices  24.3 us (2%)
  between operations  18.2 us (2%)
    dot_general x20, matrix products, weight_product(): lax.dot_general(left_side, right_side, (((0,), (0,)), ((), ())), preferre...  151 us
    reduce_scatter x1, waiting for transfers between devices, body(): lax.psum_scatter(grad_w_down, 'dp', scatter_dimension=0, tiled=True)  116 us
    dot_general x20, matrix products, transpose_product(): lax.dot_general(left_side, right_side, (((1,), (1,)), ((), ())), preferre...  90.6 us
    unnamed x1, blocking collectives  62 us
    dynamic_update_slice x30, other arithmetic, body(): lax.dynamic_update_index_in_dim(store_array, leaf_array, slot_index, 0)  54.1 us
    dot_general x5, matrix products, layer_backward(): jnp.einsum('bqhe,bkhe->bhqk', d_context, value_heads, preferred_element_t...  50.8 us
    dot_general x10, matrix products, score_block(): jnp.einsum('bqhe,bkhe->bhqk', queries, key_heads, preferred_element_type=...  50.4 us
    dot_general x5, matrix products, layer_forward(): jnp.dot(normed_low, w_up, preferred_element_type=jnp.float32) + bias_up  40.1 us
  transfers between devices with their start and end apart: 12, of which 8 were waited for; matrix products, arithmetic and copies ran while one was open for 30% of the time, Pallas kernels for 0%

commit v1 on v0

v1 whole, which is shorter than its diff:
```python
import functools

import jax
import jax.numpy as jnp
from jax import lax
from jax.experimental import pallas as pl
from jax.experimental.pallas import tpu as pltpu
from jax.sharding import PartitionSpec as P_

BF, F32 = jnp.bfloat16, jnp.float32
SEQ, D, FF, QB, NQ, KW, PAIRS = 512, 768, 3072, 128, 4, 384, 6
EPS = 1e-5
C0, C1 = 0.7978845608028654, 0.044715
FC = 512


def dot(a,b): return lax.dot_general(a,b,(((1,),(0,)),((),())),preferred_element_type=F32)


def dnt(a,b): return lax.dot_general(a,b,(((1,),(1,)),((),())),preferred_element_type=F32)


def dtn(a,b): return lax.dot_general(a,b,(((0,),(0,)),((),())),preferred_element_type=F32)


def krange(qb):
    lo=max(0,(qb-1)*QB); hi=min(SEQ,(qb+2)*QB)
    return lo,hi


def norm_rows(v):
    c=v-jnp.mean(v,axis=-1,keepdims=True)
    r=lax.rsqrt(jnp.mean(c*c,axis=-1,keepdims=True)+EPS)
    return c*r, r


def make_bias(idc, idr, bias):
    for qb in range(NQ):
        lo,hi=krange(qb)
        same=idc[lo:hi,:]==idr[:,qb*QB:(qb+1)*QB]
        bias[qb,0:hi-lo,:]=jnp.where(same,0.0,-1e30).astype(F32)
VAR=2


def f_qkv(x, wqkv, qkv):
    qkv[:,0:D]=(dot(x[...],wqkv[:,0:D])*0.125).astype(BF)
    for j in range(1,3):
        qkv[:,j*D:(j+1)*D]=dot(x[...],wqkv[:,j*D:(j+1)*D]).astype(BF)


def head_masks(rows):
    lane=lax.broadcasted_iota(jnp.int32,(rows,128),1)
    return (lane<64)


def stack_heads(q, lo_b, hi_b):
    return jnp.concatenate([q*lo_b, q*hi_b],axis=0)


def lane_bf(w):
    lane=lax.broadcasted_iota(jnp.int32,(1,128),1)
    lo=jnp.where(lane<64,1.0,0.0).astype(BF); hi=jnp.where(lane<64,0.0,1.0).astype(BF)
    return lo,hi


def f_attn(qkv, bias, P, ctx):
    lo_b,hi_b=lane_bf(128)
    first=head_masks(QB)
    def pair_body(p0,_):
        items=[(pp,qb) for pp in range(2) for qb in range(NQ)]
        S={}
        def base_of(pp): return pl.multiple_of((p0*2+pp)*128,128)
        def qk(it):
            pp,qb=it; base=base_of(pp)
            lo,hi=krange(qb)
            q=qkv[qb*QB:(qb+1)*QB,pl.ds(base,128)]
            k=qkv[lo:hi,pl.ds(pl.multiple_of(D+base,128),128)]
            S[it]=dnt(k,stack_heads(q,lo_b,hi_b))
        def rest(it):
            pp,qb=it; base=base_of(pp); p=p0*2+pp
            lo,hi=krange(qb); kw=hi-lo
            s2=S.pop(it); b=bias[qb,0:kw,:]
            pn=[]
            for hd in range(2):
                s=s2[:,hd*QB:(hd+1)*QB]+b
                m=jnp.max(s,axis=0,keepdims=True)
                e=jnp.exp(s-m)
                t=jnp.sum(e,axis=0,keepdims=True)
                pb=(e*(1.0/t)).astype(BF)
                pn.append(pb)
            pb=jnp.concatenate(pn,axis=1)
            P[p,qb,0:kw,:]=pb
            v=qkv[lo:hi,pl.ds(pl.multiple_of(2*D+base,128),128)]
            o=dtn(pb,v)
            ctx[qb*QB:(qb+1)*QB,pl.ds(base,128)]=jnp.where(first,o[:QB],o[QB:]).astype(BF)
        for i,it in enumerate(items):
            if i<2: qk(it)
        for i,it in enumerate(items):
            if i+2<len(items): qk(items[i+2])
            rest(it)
        return 0
    lax.fori_loop(0,PAIRS//2,pair_body,0)


def f_mid(x, ctx, wout, ga, sa, n1, nl, r1, nf):
    RB=256
    for rb in range(SEQ//RB):
        rs=slice(rb*RB,(rb+1)*RB)
        a=x[rs,:].astype(F32)+dot(ctx[rs,:],wout[...])
        n,r=norm_rows(a)
        y=n*ga[...]+sa[...]
        n1[rs,:]=n.astype(BF); r1[rs,:]=jnp.broadcast_to(r,(RB,128))
        nl[rs,:]=y.astype(BF); nf[rs,:]=y


def gelu_both(p):
    p2=p*p
    t=jnp.tanh(p*(C0+(C0*C1)*p2))
    h=0.5+0.5*t
    d=h+ (p*(C0+(3*C0*C1)*p2))*(0.5-0.5*(t*t))
    return p*h, d


def f_ffn(nl, nf, wup, bu, wdown, bd, gf, sf, dg, act, n2, r2, h):
    NC=FF//FC
    for c in range(NC):
        cs=slice(c*FC,(c+1)*FC)
        p=dot(nl[...],wup[:,cs])+bu[:,cs]
        a,d=gelu_both(p)
        act[:,cs]=a.astype(BF); dg[:,cs]=d.astype(BF)
    RB=256
    for rb in range(SEQ//RB):
        rs=slice(rb*RB,(rb+1)*RB)
        f=nf[rs,:]+dot(act[rs,:],wdown[...])+bd[...]
        n,r=norm_rows(f)
        n2[rs,:]=n.astype(BF); r2[rs,:]=jnp.broadcast_to(r,(RB,128))
        h[rs,:]=(n*gf[...]+sf[...]).astype(BF)


def nb(e, n, r):
    return r*(e-jnp.mean(e,axis=-1,keepdims=True)-n*jnp.mean(e*n,axis=-1,keepdims=True))


def colsum8(v):
    R=v.shape[0]
    return jnp.sum(v.reshape(R//8,8,v.shape[1]),axis=0)


def b_ffn(g, n2, r2, gf, wdown, dg, wup, n1, r1, ga, down_in, up_in, dff, datt, out_in, sm, sbu):
    RB=256
    for rb in range(SEQ//RB):
        rs=slice(rb*RB,(rb+1)*RB)
        gg=g[rs,:].astype(F32); n=n2[rs,:].astype(F32); r=r2[rs,0:1]
        d=nb(gg*gf[...],n,r)
        dl=d.astype(BF)
        down_in[rs,:]=dl; dff[rs,:]=d
        sm[3]+=colsum8(gg*n); sm[4]+=colsum8(gg); sm[2]+=colsum8(dl.astype(F32))
    for c in range(FF//FC):
        cs=slice(c*FC,(c+1)*FC)
        u=(dnt(down_in[...],wdown[cs,:])*dg[:,cs].astype(F32)).astype(BF)
        up_in[:,cs]=u
        sbu[:,cs]+=colsum8(u.astype(F32))
    for rb in range(SEQ//RB):
        rs=slice(rb*RB,(rb+1)*RB)
        gg=dff[rs,:]+dnt(up_in[rs,:],wup[...])
        n=n1[rs,:].astype(F32); r=r1[rs,0:1]
        d=nb(gg*ga[...],n,r)
        datt[rs,:]=d; out_in[rs,:]=d.astype(BF)
        sm[0]+=colsum8(gg*n); sm[1]+=colsum8(gg)


def b_attn(out_in, wout, qkv, P, ctx, dctx, dq, dlt, vacc):
    dctx[...]=dnt(out_in[...],wout[...]).astype(BF)
    lo_b,hi_b=lane_bf(128)
    first=head_masks(QB)
    row=lax.broadcasted_iota(jnp.int32,(8,128),0); lane=lax.broadcasted_iota(jnp.int32,(8,128),1)
    sel=jnp.where((lane//64)==row,1.0,0.0).astype(BF)
    def pair(p,_):
        base=pl.multiple_of(p*128,128); kb=pl.multiple_of(D+base,128); vb=pl.multiple_of(2*D+base,128)
        dof=(dctx[:,pl.ds(base,128)].astype(F32)*ctx[:,pl.ds(base,128)].astype(F32)).astype(BF)
        dl=dnt(sel,dof)
        kparts={}; vparts={}
        for qb in range(NQ):
            lo,hi=krange(qb); kw=hi-lo
            qs=slice(qb*QB,(qb+1)*QB)
            q2=stack_heads(qkv[qs,pl.ds(base,128)],lo_b,hi_b)
            v=qkv[lo:hi,pl.ds(vb,128)]
            do2=stack_heads(dctx[qs,pl.ds(base,128)],lo_b,hi_b)
            dp=dnt(v,do2)
            pn=P[p,qb,0:kw,:]
            ds=[]
            for hd in range(2):
                hs=slice(hd*QB,(hd+1)*QB)
                ds.append((pn[:,hs].astype(F32)*(dp[:,hs]-dl[hd:hd+1,qs])).astype(BF))
            ds=jnp.concatenate(ds,axis=1)
            k=qkv[lo:hi,pl.ds(kb,128)]
            dqq=dtn(ds,k)
            dq[qs,pl.ds(base,128)]=(jnp.where(first,dqq[:QB],dqq[QB:])*0.125).astype(BF)
            dk=dot(ds,q2); dv=dot(pn,do2)
            for b in range(lo//QB,hi//QB):
                sl=slice(b*QB-lo,(b+1)*QB-lo)
                kparts[b]=dk[sl] if b not in kparts else kparts[b]+dk[sl]
                vparts[b]=dv[sl] if b not in vparts else vparts[b]+dv[sl]
            if qb>=1:
                b=qb-1
                dq[b*QB:(b+1)*QB,pl.ds(kb,128)]=kparts.pop(b).astype(BF); dq[b*QB:(b+1)*QB,pl.ds(vb,128)]=vparts.pop(b).astype(BF)
        b=NQ-1
        dq[b*QB:(b+1)*QB,pl.ds(kb,128)]=kparts.pop(b).astype(BF); dq[b*QB:(b+1)*QB,pl.ds(vb,128)]=vparts.pop(b).astype(BF)
        return 0
    lax.fori_loop(0,PAIRS,pair,0)
PSH=(6,4,384,256)
BSH=(4,384,128)


def b_in(dq, wqkv, datt, din):
    RB=256
    for rb in range(SEQ//RB):
        rs=slice(rb*RB,(rb+1)*RB)
        din[rs,:]=(datt[rs,:]+dnt(dq[rs,:],wqkv[...])).astype(BF)


SAVED = ("qkv", "P", "ctx", "n1", "r1", "nl", "dg", "act", "n2", "r2")
RELOADED = ("qkv", "P", "ctx", "n1", "r1", "dg", "n2", "r2")
ROWS = ("down_in", "up_in", "out_in", "dq")
SHAPES = dict(
    qkv=((SEQ, 3 * D), BF), P=((PAIRS, NQ, KW, 2 * QB), BF), ctx=((SEQ, D), BF), n1=((SEQ, D), BF), r1=((SEQ, 128), F32),
    nl=((SEQ, D), BF), dg=((SEQ, FF), BF), act=((SEQ, FF), BF), n2=((SEQ, D), BF), r2=((SEQ, 128), F32),
    down_in=((SEQ, D), BF), up_in=((SEQ, FF), BF), out_in=((SEQ, D), BF), dq=((SEQ, 3 * D), BF),
)
IN_NAMES = ("tokens", "cot", "idc", "idr", "wqkv_h", "wout_h", "wup_h", "wdown_h", "ga", "sa", "bu", "bd", "gf", "sf")
OUT_NAMES = ("h_all", "din_all", "sm", "sbu", "x_all") + tuple("s_" + k for k in SAVED) + tuple("s_" + k for k in ROWS)
SCRATCH = dict(
    io=((8, SEQ, D), BF), wqkv=((D, 3 * D), BF), wout=((D, D), BF), wup=((D, FF), BF), wdown=((FF, D), BF),
    nf=((SEQ, D), F32), datt=((SEQ, D), F32), dctx=((SEQ, D), BF), ho=((SEQ, D), BF), din=((SEQ, D), BF),
    bias=((NQ, KW, QB), F32), **SHAPES,
)


def pipeline_kernel(micro, *refs):
    names = IN_NAMES + OUT_NAMES + tuple(SCRATCH) + ("sem_w", "sem_own", "sem_f", "sem_l", "sem_b", "sem_x", "sem_ho", "sem_din", "send_h", "send_d", "recv")
    r = dict(zip(names, refs))
    sec = lax.axis_index("section")
    dp = lax.axis_index("dp")
    first_sec = sec == 0
    partner = (1 - sec, dp)
    barrier = pltpu.get_barrier_semaphore()
    pl.semaphore_signal(barrier, inc=1, device_id=partner, device_id_type=pl.DeviceIdType.MESH)

    def own_copy(src):
        return pltpu.make_async_copy(src, r["io"].at[pl.ds(0, micro)], r["sem_own"])

    weights = ("wqkv", "wout", "wup", "wdown")
    w_copies = [pltpu.make_async_copy(r[k + "_h"], r[k], r["sem_w"].at[i]) for i, k in enumerate(weights)]

    @pl.when(first_sec)
    def _():
        own_copy(r["tokens"]).start()

    @pl.when(jnp.logical_not(first_sec))
    def _():
        own_copy(r["cot"]).start()

    for c in w_copies:
        c.start()
    r["sm"][...] = jnp.zeros_like(r["sm"])
    r["sbu"][...] = jnp.zeros_like(r["sbu"])
    own_copy(r["tokens"]).wait()
    for c in w_copies:
        c.wait()
    pl.semaphore_wait(barrier, 1)

    def save(k, mb):
        return pltpu.make_async_copy(r[k], r["s_" + k].at[mb], r["sem_f"].at[SAVED.index(k)])

    def load(k, mb):
        return pltpu.make_async_copy(r["s_" + k].at[mb], r[k], r["sem_l"].at[RELOADED.index(k)])

    def save_rows(k, mb):
        return pltpu.make_async_copy(r[k], r["s_" + k].at[mb], r["sem_b"].at[ROWS.index(k)])

    def save_x(mb):
        return pltpu.make_async_copy(r["io"].at[mb + micro * sec], r["x_all"].at[mb], r["sem_x"])

    def save_h(mb):
        return pltpu.make_async_copy(r["ho"], r["h_all"].at[mb], r["sem_ho"])

    def save_din(mb):
        return pltpu.make_async_copy(r["din"], r["din_all"].at[mb], r["sem_din"])

    def send(k, mb, sem):
        return pltpu.make_async_remote_copy(
            src_ref=r[k], dst_ref=r["io"].at[micro + mb], send_sem=r[sem], recv_sem=r["recv"].at[mb],
            device_id=partner, device_id_type=pl.DeviceIdType.MESH,
        )

    EARLY_BOTH, EARLY_ONE = ("ctx", "nl"), ("qkv", "P", "n1", "r1")
    LATE_BOTH, LATE_ONE = ("act",), ("dg", "n2", "r2")

    def step(t, carry):
        is_f = jnp.where(first_sec, t < micro, lax.rem(t, 2) == 0)
        mb = jnp.where(first_sec, lax.rem(t, micro), lax.div(t, 2))
        after_f = jnp.where(first_sec, (t >= 1) & (t <= micro), lax.rem(t, 2) == 1)
        prev = jnp.where(first_sec, lax.rem(t + micro - 1, micro), lax.div(t, 2))

        def wait_late():
            for k in LATE_BOTH:
                save(k, prev).wait()
            save_h(prev).wait()

            @pl.when(first_sec)
            def _():
                for k in LATE_ONE:
                    save(k, prev).wait()
                send("ho", prev, "send_h").wait_send()

        @pl.when(after_f)
        def _():
            for k in EARLY_BOTH:
                save(k, prev).wait()
            save_x(prev).wait()

            @pl.when(first_sec)
            def _():
                for k in EARLY_ONE:
                    save(k, prev).wait()

        @pl.when(is_f)
        def _():
            rows = pl.ds(pl.multiple_of(mb * SEQ, SEQ), SEQ)
            make_bias(r["idc"].at[rows], r["idr"].at[mb], r["bias"])

            @pl.when(jnp.logical_not(first_sec))
            def _():
                send("ho", mb, "send_h").wait_recv()

            save_x(mb).start()
            x = r["io"].at[mb + micro * sec]
            f_qkv(x, r["wqkv"], r["qkv"])

            @pl.when(first_sec)
            def _():
                save("qkv", mb).start()

            f_attn(r["qkv"], r["bias"], r["P"], r["ctx"])
            save("ctx", mb).start()

            @pl.when(first_sec)
            def _():
                save("P", mb).start()

            f_mid(x, r["ctx"], r["wout"], r["ga"], r["sa"], r["n1"], r["nl"], r["r1"], r["nf"])
            save("nl", mb).start()

            @pl.when(first_sec)
            def _():
                save("n1", mb).start()
                save("r1", mb).start()

            @pl.when(after_f)
            def _():
                wait_late()

            f_ffn(r["nl"], r["nf"], r["wup"], r["bu"], r["wdown"], r["bd"], r["gf"], r["sf"], r["dg"], r["act"], r["n2"], r["r2"], r["ho"])
            save("act", mb).start()
            save_h(mb).start()

            @pl.when(first_sec)
            def _():
                send("ho", mb, "send_h").start()
                for k in LATE_ONE:
                    save(k, mb).start()

        @pl.when(jnp.logical_not(is_f))
        def _():
            @pl.when(first_sec)
            def _():
                @pl.when(after_f)
                def _():
                    wait_late()
                    for k in RELOADED:
                        load(k, mb).start()

                send("din", mb, "send_d").wait_recv()
                for k in RELOADED:
                    load(k, mb).wait()

            not_first_b = jnp.where(first_sec, t > micro, t > 1)
            before = mb - 1

            @pl.when(not_first_b)
            def _():
                for k in ROWS:
                    save_rows(k, before).wait()
                save_din(before).wait()

                @pl.when(jnp.logical_not(first_sec))
                def _():
                    send("din", before, "send_d").wait_send()

            g = r["io"].at[mb + micro * (1 - sec)]
            b_ffn(g, r["n2"], r["r2"], r["gf"], r["wdown"], r["dg"], r["wup"], r["n1"], r["r1"], r["ga"], r["down_in"], r["up_in"], r["nf"], r["datt"], r["out_in"], r["sm"], r["sbu"])
            for k in ROWS[:3]:
                save_rows(k, mb).start()

            @pl.when(jnp.logical_not(first_sec))
            def _():
                wait_late()

            b_attn(r["out_in"], r["wout"], r["qkv"], r["P"], r["ctx"], r["dctx"], r["dq"], None, None)
            save_rows("dq", mb).start()
            b_in(r["dq"], r["wqkv"], r["datt"], r["din"])
            save_din(mb).start()

            @pl.when(jnp.logical_not(first_sec))
            def _():
                send("din", mb, "send_d").start()

            @pl.when(first_sec & (mb < micro - 1))
            def _():
                for k in RELOADED:
                    load(k, mb + 1).start()

        return carry

    lax.fori_loop(0, 2 * micro, step, 0)
    last = micro - 1
    for k in ROWS:
        save_rows(k, last).wait()
    save_din(last).wait()

    @pl.when(jnp.logical_not(first_sec))
    def _():
        send("din", last, "send_d").wait_send()


def run_pipeline(tokens, cot, comb, weights, micro):
    w_qkv, w_out, gain_attn, shift_attn, w_up, bias_up, w_down, bias_down, gain_ffn, shift_ffn = weights
    any_space, vmem = pl.BlockSpec(memory_space=pl.ANY), pl.BlockSpec(memory_space=pltpu.VMEM)
    operands = (
        tokens.reshape(micro, SEQ, D), cot.reshape(micro, SEQ, D), comb.reshape(micro * SEQ, 1), comb.reshape(micro, 1, SEQ),
        w_qkv, w_out, w_up, w_down, gain_attn, shift_attn, bias_up, bias_down, gain_ffn, shift_ffn,
    )
    in_specs = [any_space] * 2 + [vmem] * 2 + [any_space] * 4 + [vmem] * 6
    out_shape = [
        jax.ShapeDtypeStruct((micro, SEQ, D), BF), jax.ShapeDtypeStruct((micro, SEQ, D), BF),
        jax.ShapeDtypeStruct((5, 8, D), F32), jax.ShapeDtypeStruct((8, FF), F32), jax.ShapeDtypeStruct((micro, SEQ, D), BF),
    ] + [jax.ShapeDtypeStruct((micro,) + SHAPES[k][0], SHAPES[k][1]) for k in SAVED + ROWS]
    out_specs = [any_space] * 2 + [vmem] * 2 + [any_space] * (len(out_shape) - 4)
    dma = pltpu.SemaphoreType.DMA
    scratch = [pltpu.VMEM(*SCRATCH[k]) for k in SCRATCH] + [
        dma((4,)), dma, dma((len(SAVED),)), dma((len(RELOADED),)), dma((len(ROWS),)), dma, dma, dma, dma, dma, dma((micro,)),
    ]
    outs = pl.pallas_call(
        functools.partial(pipeline_kernel, micro), out_shape=out_shape, in_specs=in_specs, out_specs=out_specs, scratch_shapes=scratch,
        name="pipeline",
        compiler_params=pltpu.CompilerParams(collective_id=1, has_side_effects=True, vmem_limit_bytes=62 * 2**20),
    )(*operands)
    return dict(zip(OUT_NAMES, outs))


def weight_product(left, right):
    rows = left.shape[0] * left.shape[1]
    return lax.dot_general(
        left.reshape(rows, -1), right.reshape(rows, -1), (((0,), (0,)), ((), ())), preferred_element_type=F32
    )


def body(
    tokens, cotangent, segment_ids, feature_ids, w_qkv, w_out, gain_attn, shift_attn, w_up, bias_up, w_down, bias_down, gain_ffn, shift_ffn
):
    sec = lax.axis_index("section")
    micro = segment_ids.shape[0]
    comb = segment_ids * 128 + feature_ids * (1 - sec)
    weights = (w_qkv[0], w_out[0], gain_attn, shift_attn, w_up[0], bias_up, w_down[0], bias_down, gain_ffn, shift_ffn)
    o = run_pipeline(tokens, cotangent, comb, weights, micro)
    sm = jnp.sum(o["sm"], axis=1)
    sbu = jnp.sum(o["sbu"], axis=0)
    scatter = lambda v: lax.psum_scatter(v, "dp", scatter_dimension=0, tiled=True)[None]
    g_qkv = scatter(weight_product(o["x_all"], o["s_dq"]))
    g_out = scatter(weight_product(o["s_ctx"], o["s_out_in"]))
    g_up = scatter(weight_product(o["s_nl"], o["s_up_in"]))
    g_down = scatter(weight_product(o["s_act"], o["s_down_in"]))
    return (
        o["h_all"].reshape(1, micro * SEQ, D), o["din_all"].reshape(1, micro * SEQ, D), g_qkv, g_out, scatter(sm[0]), scatter(sm[1]),
        g_up, scatter(sbu), g_down, scatter(sm[2]), scatter(sm[3]), scatter(sm[4]),
    )


def solution(mesh):
    rows, mat, vec = P_("dp", None), P_("section", None, None), P_("section", None)
    in_specs = (rows,) * 4 + (mat, mat, vec, vec, mat, vec, mat, vec, vec, vec)
    big, small = P_("section", "dp", None), P_("section", "dp")
    out_specs = (big, big, big, big, small, small, big, small, big, small, small, small)
    return jax.shard_map(body, mesh=mesh, in_specs=in_specs, out_specs=out_specs, check_vma=False)
```

time: 1130 us -> 634 us (0.56)
  matrix products: 508 us -> 50.8 us
  Pallas kernels: 0 us -> 216 us
  other arithmetic: 172 us -> 0.79 us
  local copies, waits for them, and re-layouts: 166 us -> 14.3 us
  waiting for transfers between devices: 173 us -> 276 us
  starting transfers between devices: 24.3 us -> 0.16 us
    dot_general x95 -> x4, matrix products: 508 us -> 50.8 us  [weight_product(): lax.dot_general(left.reshape(rows, -1), right.reshape(rows, -1), (((0,),...]
    pallas_call x0 -> x1, Pallas kernels: none -> 216 us  [run_pipeline(): pl.pallas_call(functools.partial(pipeline_kernel, micro), out_shape=out_s...]
    reduce_scatter x4, waiting for transfers between devices: 137 us -> 276 us  [body(): lax.psum_scatter(v, 'dp', scatter_dimension=0, tiled=True)[None]]
    dynamic_update_slice x35 -> x0, other arithmetic: 62.5 us -> none  [the longest x30 54.1 us: body(): lax.dynamic_update_index_in_dim(store_array, leaf_array, slot_index, 0)]
    reduce_sum x25 -> x2, other arithmetic: 48.4 us -> 0.07 us  [the longest x1 0.04 us: body(): sm = jnp.sum(o['sm'], axis=1)]
    broadcast_in_dim x14 -> x3, local copies, waits for them, and re-layouts: 40.9 us -> 1.75 us  [body(): lax.psum_scatter(v, 'dp', scatter_dimension=0, tiled=True)[None]]
    convert_element_type x5 -> x0, other arithmetic: 36.9 us -> none  [layer_backward(): (prob_full * (d_prob - jnp.sum(d_prob * prob_full, axis=-1, keepdims=True...]
    ppermute x8 -> x0, waiting for transfers between devices: 35.5 us -> none  [from_behind(): lax.ppermute(value, axis, [(source, source + steps) for source in range(f...]
  transfers between devices with their start and end apart: 12 -> 4, of which waited for: 8 -> 3; matrix products, arithmetic and copies ran while one was open for 30% -> 7% of each run, Pallas kernels for 0% -> 0%
where the time goes in v1:
time: 634 us
  waiting for transfers between devices  276 us (44%)
  Pallas kernels  216 us (34%)
  blocking collectives  60.4 us (10%)
  matrix products  50.8 us (8%)
  between operations  15.5 us (2%)
  local copies, waits for them, and re-layouts  14.3 us (2%)
    reduce_scatter x4, waiting for transfers between devices, body(): lax.psum_scatter(v, 'dp', scatter_dimension=0, tiled=True)[None]  276 us
    pallas_call x1, Pallas kernels, run_pipeline(): pl.pallas_call(functools.partial(pipeline_kernel, micro), out_shape=out_s...  216 us
    unnamed x1, blocking collectives  60.4 us
    dot_general x4, matrix products, weight_product(): lax.dot_general(left.reshape(rows, -1), right.reshape(rows, -1), (((0,),...  50.8 us
  transfers between devices with their start and end apart: 4, of which 3 were waited for; matrix products, arithmetic and copies ran while one was open for 7% of the time, Pallas kernels for 0%

profile of v1, /device:TPU:0, one launch (start us, length us, event | category | flops | bytes accessed | tf_op | source)
XLA Modules:
  0.0 634.1 jit_solution(15393302559745659834)
XLA Ops:
  7.2 0.7 multiply_add_fusion
  7.9 0.6 reshape.53.refs_3_
  8.6 1.3 copy.41
  9.9 216.1 %pipeline.1 = (bf16[4,512,768]{2,1,0:T(8,128)(2,1)}, bf16[4,512,768]{2,1,0:T(8,128)(2,1)}, f32[5,8,768]{2,1,0:T(8,128)}, f32[8,3072]{1,0:T(8,128)}, bf16[4,512,7...) custom-call(bf16[4,512,768]{2,1,0:T(8,128)(2,1)} %bitcast.50, ...), custom_call_target="tpu_custom_call" | custom-call | tf_op jit(solution)/shard_map/pipeline/pallas_call | solution.py:453
  226.0 7.1 %convolution_bitcast_fusion.3 = f32[768,768]{1,0:T(8,128)} fusion(bf16[4,512,768]{2,1,0:T(8,128)(2,1)} %get-tuple-element.28, bf16[4,512,768]{2,1,0:T(8,128)(2,1)} %get-tuple-element.29), kind=kOutput, calls=%fused_computation.3 | convolution fusion | flops 2415919104 | bytes 8650752 | tf_op jit(solution)/shard_map/dot_general | solution.py:463
  233.2 12.8 %convolution_bitcast_fusion.1 = f32[768,2304]{1,0:T(8,128)} fusion(bf16[4,512,768]{2,1,0:T(8,128)(2,1)S(1)} %copy-done.6, bf16[4,512,2304]{2,1,0:T(8,128)(2,1)} %get-tuple-element.27), kind=kOutput, calls=%fused_computation.1 | convolution fusion | flops 7247757312 | bytes 19660800 | tf_op jit(solution)/shard_map/dot_general | solution.py:463
  246.1 1.9 copy-done.5
  248.0 15.6 %convolution_bitcast_fusion = f32[3072,768]{1,0:T(8,128)} fusion(bf16[4,512,3072]{2,1,0:T(8,128)(2,1)} %get-tuple-element.34, bf16[4,512,768]{2,1,0:T(8,128)(2,1)S(1)} %copy-done.5), kind=kOutput, calls=%fused_computation | convolution fusion | flops 9663676416 | bytes 25165824 | tf_op jit(solution)/shard_map/dot_general | solution.py:463
  263.6 0.0 reduce-scatter.9.cloned.1.call-start
  263.7 1.8 copy-done.4
  265.5 15.3 %convolution_bitcast_fusion.2 = f32[768,3072]{1,0:T(8,128)} fusion(bf16[4,512,768]{2,1,0:T(8,128)(2,1)S(1)} %copy-done.4, bf16[4,512,3072]{2,1,0:T(8,128)(2,1)} %get-tuple-element.32), kind=kOutput, calls=%fused_computation.2 | convolution fusion | flops 9663676416 | bytes 25165824 | tf_op jit(solution)/shard_map/dot_general | solution.py:463
  280.8 0.9 copy-done.2
  281.8 0.6 dynamic-slice
  283.7 60.4 %all-reduce.6 = (f32[768]{0:T(1024)S(1)}, f32[768]{0:T(1024)S(1)}, f32[3072]{0:T(1024)S(1)}, f32[768]{0:T(1024)S(1)}, f32[768]{0:T(1024)S(1)}, /*index=5*/f32[768]{0:T(1024)S(1)}) all-reduce(f32[768]{0:T(1024)S(1)} %get-tuple-element.40, f32[768]{0:T(1024)S(1)} %get-tuple-element.39, ...), channel_id=4, replica_groups=mesh['section'=2,'dp'=16] {'dp'}, use_global_device_ids=true, to_apply=%region_3.0.clone | all-reduce | flops 6912 | bytes 55296
  344.2 0.6 dynamic-slice.5
  344.8 0.6 dynamic-slice_bitcast_fusion.4
  345.4 0.6 dynamic-slice_bitcast_fusion
  346.0 0.6 dynamic-slice_bitcast_fusion.2
  346.5 44.2 %reduce-scatter.5.cloned.1.call-done = f32[48,2304]{1,0:T(8,128)} async-done(((f32[768,2304]{1,0:T(8,128)}), f32[48,2304]{1,0:T(8,128)}) %reduce-scatter.5.cloned.1.call-update) | async-done | bytes 442384 | tf_op jit(solution)/shard_map/reduce_scatter | solution.py:478
  390.7 115.6 %reduce-scatter.11.cloned.1.call-done = f32[192,768]{1,0:T(8,128)} async-done(((f32[3072,768]{1,0:T(8,128)}), f32[192,768]{1,0:T(8,128)}) %reduce-scatter.11.cloned.1.call-update) | async-done | bytes 589840 | tf_op jit(solution)/shard_map/reduce_scatter | solution.py:478
  506.3 116.2 %reduce-scatter.9.cloned.1.call-done = f32[48,3072]{1,0:T(8,128)} async-done(((f32[768,3072]{1,0:T(8,128)}), f32[48,3072]{1,0:T(8,128)}) %reduce-scatter.9.cloned.1.call-update) | async-done | bytes 589840 | tf_op jit(solution)/shard_map/reduce_scatter | solution.py:478
  622.6 1.7 copy.44
  624.2 1.4 copy-done
  625.6 1.7 copy.45
  (24 shorter events, 0.3 us)
Async XLA Ops:
  7.2 339.4 %reduce-scatter.7.cloned.1.call-start = ((), (), s32[]{:S(2)}) async-start(), calls=%async_computation.5 | async-start | bytes 2506752 | tf_op jit(solution)/shard_map/reduce_scatter | solution.py:478
  226.0 7.1 %copy-start.6 = (bf16[4,512,768]{2,1,0:T(8,128)(2,1)S(1)}, bf16[4,512,768]{2,1,0:T(8,128)(2,1)}, u32[]{:S(2)}) copy-start(bf16[4,512,768]{2,1,0:T(8,128)(2,1)} %get-tuple-element.26) | copy-start | bytes 9437188
  233.1 157.6 %reduce-scatter.5.cloned.1.call-start = ((), (), s32[]{:S(2)}) async-start(), calls=%async_computation.4 | async-start | bytes 7520256 | tf_op jit(solution)/shard_map/reduce_scatter | solution.py:478
  246.0 2.0 copy-start.5
  246.0 260.3 %reduce-scatter.11.cloned.1.call-start = ((), (), s32[]{:S(2)}) async-start(), calls=%async_computation.7 | async-start | bytes 10027008 | tf_op jit(solution)/shard_map/reduce_scatter | solution.py:478
  263.6 1.9 copy-start.4
  263.6 358.9 %reduce-scatter.9.cloned.1.call-start = ((), (), s32[]{:S(2)}) async-start(), calls=%async_computation.6 | async-start | bytes 10027008 | tf_op jit(solution)/shard_map/reduce_scatter | solution.py:478
  280.8 0.9 copy-start.2
  280.8 0.9 copy-start.3
  280.8 1.0 copy-start.7
  280.8 341.8 %copy-start.1 = (bf16[4,512,768]{2,1,0:T(8,128)(2,1)S(1)}, bf16[4,512,768]{2,1,0:T(8,128)(2,1)}, u32[]{:S(2)}) copy-start(bf16[4,512,768]{2,1,0:T(8,128)(2,1)} %get-tuple-element.24) | copy-start | bytes 9437188
  622.6 3.0 copy-start
Sparse Core Ops, SparseCore 0:
  233.2 63.2 reduce-scatter.6
  301.6 89.0 reduce-scatter.4
  395.4 110.8 reduce-scatter.10
  511.4 111.1 reduce-scatter.8
